TPU v7x, 512 devices: a whole 4x4x16 slice. The times are simulated.
512 devices in a mesh: blk: 32 (over z_lo, x), grp: 16 (over z_hi, y, core).
Axes of the slice: x: 4, y: 4, z: 16 (z_hi: 2, z_lo: 8; z = z_hi * 8 + z_lo), core: 2. Of those that a mesh axis runs over, the one named last changes fastest.
Arguments:
- positions: float32 [3, 32768], P(None, ('blk', 'grp')), may hold values from -0.25 to 31.25, as said below
- moments: float32 [2, 2, 3, 32768], P(None, None, None, ('blk', 'grp')), may hold values from -6 to 6
- inv_polar_re: float32 [32768], P(('blk', 'grp')), may hold values from 0.5 to 2
- inv_polar_im: float32 [32768], P(('blk', 'grp')), may hold values from -0.5 to 0.5
- mode_field: float32 [2, 3, 32768, 512], P(None, None, ('blk', 'grp')), may hold values from -0.0390625 to 0.0390625
- mode_detune: float32 [512], replicated, may hold values from -1 to 1
- mode_width: float32 [512], replicated, may hold values from 0.05 to 1
Outputs:
- response: float32 [2, 2, 3, 32768], P(None, None, None, ('blk', 'grp'))
Inputs may be any that keep to these rules, and one draw needn't show every extreme that they name: `positions`: dipole n lies within 0.25, in each coordinate, of the lattice site (n % 32, (n // 32) % 32, n // 1024); distinct dipoles are at least 0.5 apart.
All inputs are finite; a program needn't handle non-finite values.
Results may differ from a plain program's by a relative error of at most 0.0003.
Values sent between devices are 32-bit elements; how exact they have to be, the bound alone decides.
A program may use at most 64 MiB of HBM per device.

v0:
```python
import math
import jax
import jax.numpy as jnp
from jax import lax
from jax.sharding import Mesh
from jax.sharding import PartitionSpec as P

BLK_GRP = ("blk_0", "blk_1", "grp_0", "grp_1", "grp_2")
GRP = ("grp_0", "grp_1", "grp_2")
BLK = ("blk_0", "blk_1")
wavenumber = 1.0
coupling = 0.05
near_limit = 0.04


def over_axes(value, axes):
    for axis in axes:
        value = lax.psum(value, axis)
    return value


def laid_out(tiles, dim):
    tiles = jnp.moveaxis(tiles, 0, dim)
    shape = tiles.shape
    return tiles.reshape(*shape[:dim], shape[dim] * shape[dim + 1], *shape[dim + 2 :])


def gather_in_order(value, axes, sequence):
    tiles = value[None]
    for k in sequence:
        tiles = lax.all_gather(tiles, axes[k], axis=0, tiled=True)
    block = [lax.axis_size(axes[k]) for k in reversed(sequence)]
    tiles = tiles.reshape(*block, *value.shape)
    turned = sorted(range(len(sequence)), key=lambda place: sequence[len(sequence) - 1 - place])
    return tiles.transpose(*turned, *range(len(sequence), tiles.ndim)).reshape(-1, *value.shape)


def whole_of(value, axes, sequence, dim):
    return laid_out(gather_in_order(value, axes, sequence), dim)


def sent_to_all(value, axis):
    devices = lax.axis_size(axis)
    return lax.all_to_all(
        jnp.broadcast_to(value[None], (devices, *value.shape)), axis, 0, 0, tiled=True
    )


def gather_directly(value, axis, dim):
    return laid_out(sent_to_all(value, axis), dim)


def sent_together(arrays, axis, dim, along):
    ends, at = ([], 0)
    for a in arrays[:-1]:
        at += a.shape[along]
        ends.append(at)
    both = jnp.concatenate(arrays, axis=along)
    return tuple(jnp.split(gather_directly(both, axis, dim), ends, axis=along))


def cut_along(value, dim, devices):
    before, after = (value.shape[:dim], value.shape[dim + 1 :])
    return jnp.moveaxis(value.reshape(*before, devices, -1, *after), dim, 0)


def sent_and_summed(value, axis, dim):
    tiles = cut_along(value, dim, lax.axis_size(axis))
    arrived = lax.all_to_all(tiles, axis, split_axis=0, concat_axis=0, tiled=True)
    return arrived.sum(axis=0)


def pair_field(deltas, dipoles, axis_sum):
    delta_x, delta_y, delta_z = deltas
    square = delta_x * delta_x + delta_y * delta_y + delta_z * delta_z
    coincide = square < near_limit
    safe_square = jnp.where(coincide, 1.0, square)
    inverse = 1.0 / jnp.sqrt(safe_square)
    phase_arg = wavenumber * safe_square * inverse
    cos_val = jnp.cos(phase_arg)
    sine_val = jnp.sin(phase_arg)
    masked_cube = jnp.where(coincide, 0.0, inverse * inverse * inverse)
    near_re = phase_arg * phase_arg - 1.0
    far_re = 3.0 - phase_arg * phase_arg
    diag_re = (cos_val * near_re - sine_val * phase_arg) * masked_cube
    diag_im = (sine_val * near_re + cos_val * phase_arg) * masked_cube
    scaled = masked_cube / safe_square
    outer_re = (cos_val * far_re + 3.0 * sine_val * phase_arg) * scaled
    outer_im = (sine_val * far_re - 3.0 * cos_val * phase_arg) * scaled
    tile_list = []
    for drive_set in range(len(dipoles) // 6):
        moment_re = dipoles[6 * drive_set : 6 * drive_set + 3]
        moment_im = dipoles[6 * drive_set + 3 : 6 * drive_set + 6]
        proj_re = delta_x * moment_re[0] + delta_y * moment_re[1] + delta_z * moment_re[2]
        proj_im = delta_x * moment_im[0] + delta_y * moment_im[1] + delta_z * moment_im[2]
        along_re = outer_re * proj_re - outer_im * proj_im
        along_im = outer_re * proj_im + outer_im * proj_re
        for component in range(3):
            tile_list.append(
                diag_re * moment_re[component]
                - diag_im * moment_im[component]
                + deltas[component] * along_re
            )
        for component in range(3):
            tile_list.append(
                diag_re * moment_im[component]
                + diag_im * moment_re[component]
                + deltas[component] * along_im
            )
    return jnp.stack([jnp.sum(entry_tile, axis=axis_sum) for entry_tile in tile_list])


def contract(left, right):
    return lax.dot_general(left, right, (((0,), (1,)), ((), ())), precision=lax.Precision.HIGHEST)


def modal_project(mode_rows, moment_rows):
    amp_re = contract(mode_rows[0], moment_rows[:, 0]) - contract(mode_rows[1], moment_rows[:, 1])
    amp_im = contract(mode_rows[0], moment_rows[:, 1]) + contract(mode_rows[1], moment_rows[:, 0])
    return (amp_re, amp_im)


def spread(weights, rows):
    return lax.dot_general(weights, rows, (((0,), (1,)), ((), ())), precision=lax.Precision.HIGHEST)


def modal_spread(mode_rows, amp_re, amp_im, mode_detune, mode_width):
    denominator = mode_detune * mode_detune + mode_width * mode_width
    resp_re = (mode_detune / denominator)[:, None]
    resp_im = (mode_width / denominator)[:, None]
    weighted_re = resp_re * amp_re - resp_im * amp_im
    weighted_im = resp_re * amp_im + resp_im * amp_re
    out_re = spread(weighted_re, mode_rows[0]) - spread(weighted_im, mode_rows[1])
    out_im = spread(weighted_re, mode_rows[1]) + spread(weighted_im, mode_rows[0])
    return jnp.stack([out_re, out_im], axis=1)


def combine(moments, inv_polar_re, inv_polar_im, pair_part, modal_part):
    drives = moments.shape[0]
    dipole_count = moments.shape[3]
    field_sum = coupling * pair_part.reshape(drives, 2, 3, dipole_count) + modal_part.reshape(
        drives, 2, 3, dipole_count
    )
    moment_re = moments[:, 0]
    moment_im = moments[:, 1]
    resp_re = inv_polar_re * moment_re - inv_polar_im * moment_im - field_sum[:, 0]
    resp_im = inv_polar_re * moment_im + inv_polar_im * moment_re - field_sum[:, 1]
    return jnp.stack([resp_re, resp_im], axis=1)


def on_device(positions, moments, inv_polar_re, inv_polar_im, mode_field, mode_detune, mode_width):
    drives = moments.shape[0]
    dipole_count = positions.shape[1]
    flat_moments = moments.reshape(drives * 6, dipole_count)
    mode_rows = mode_field.reshape(2, 3 * dipole_count, mode_field.shape[3])
    amp_re, amp_im = modal_project(mode_rows, moments.reshape(drives, 2, 3 * dipole_count))
    amp_re, amp_im = (over_axes(amp_re, BLK_GRP), over_axes(amp_im, BLK_GRP))
    modal_part = modal_spread(mode_rows, amp_re, amp_im, mode_detune, mode_width).reshape(
        drives * 6, dipole_count
    )
    group_pos = whole_of(positions, (("grp_0", "grp_1"), "grp_2"), (0, 1), 1)
    initial = jnp.zeros((drives * 6, group_pos.shape[1]), jnp.float32)
    places, dipoles = sent_together((positions, flat_moments), BLK, 1, 0)
    columns = places.shape[1]
    block_width = math.gcd(columns, 256)

    def advance(block, inner):
        source_pos = lax.dynamic_slice_in_dim(places, block * block_width, block_width, 1)
        source_mom = lax.dynamic_slice_in_dim(dipoles, block * block_width, block_width, 1)
        deltas = [group_pos[axis_c][None, :] - source_pos[axis_c][:, None] for axis_c in range(3)]
        return inner + pair_field(
            deltas, [source_mom[member][:, None] for member in range(drives * 6)], 0
        )

    partial_value = lax.fori_loop(0, columns // block_width, advance, initial)
    pair_part = sent_and_summed(partial_value, GRP, 1)
    return combine(moments, inv_polar_re, inv_polar_im, pair_part, modal_part)


def solution(mesh):
    torus = Mesh(mesh.devices.reshape(8, 4, 2, 4, 2), ("blk_0", "blk_1", "grp_0", "grp_1", "grp_2"))
    placed = (
        P(None, BLK_GRP),
        P(None, None, None, BLK_GRP),
        P(BLK_GRP),
        P(BLK_GRP),
        P(None, None, BLK_GRP, None),
        P(),
        P(),
    )
    return jax.shard_map(
        on_device,
        mesh=torus,
        in_specs=placed,
        out_specs=P(None, None, None, BLK_GRP),
        check_vma=False,
    )
```

profile of v0, /device:TPU:1, one launch (start us, length us, event | category | flops | bytes accessed | tf_op | source)
XLA Modules:
  0.0 260.5 jit_solution(8766813554993038770)
XLA Ops:
  0.0 0.8 copy.39
  0.8 0.7 pad_maximum_fusion
  1.5 0.8 reshape.63
  2.3 15.9 %all-to-all-start = ((f32[32,1,960]{2,1,0:T(1,128)}), f32[32,1,960]{2,1,0:T(1,128)S(1)}, u32[]{:S(2)}, u32[]{:S(2)}) async-start(f32[32,1,960]{2,1,0:T(1,128)} %reshape.63), calls=%async_computation | async-start | bytes 262144 | tf_op jit(solution)/shard_map/all_to_all | solution.py:44
  18.4 0.3 fusion.49
  18.8 0.3 fusion.53
  19.1 0.3 convolution_add_fusion
  19.4 0.3 convolution_subtract_fusion
  19.7 29.8 %all-reduce = (f32[512,2]{0,1:T(2,128)S(1)}, f32[512,2]{0,1:T(2,128)S(1)}) all-reduce(f32[512,2]{0,1:T(2,128)S(1)} %convolution_add_fusion, f32[512,2]{0,1:T(2,128)S(1)} %convolution_subtract_fusion), channel_id=1, replica_groups=mesh['blk_0'=8,'blk_1'=4,'grp_0'=2,'grp_1'=4,'grp_2'=2] {'blk_0'}, use_global_device_ids=true, to_apply=%region_20.0 | all-reduce | flops 2048 | bytes 16384 | tf_op jit(solution)/shard_map/psum | solution.py:18
  49.5 8.5 %all-reduce.2 = (f32[512,2]{0,1:T(2,128)S(1)}, f32[512,2]{0,1:T(2,128)S(1)}) all-reduce(f32[512,2]{0,1:T(2,128)S(1)} %get-tuple-element.184, f32[512,2]{0,1:T(2,128)S(1)} %get-tuple-element.185), channel_id=1, replica_groups=mesh['blk_0'=8,'blk_1'=4,'grp_0'=2,'grp_1'=4,'grp_2'=2] {'blk_1'}, use_global_device_ids=true, to_apply=%region_21.0 | all-reduce | flops 2048 | bytes 16384 | tf_op jit(solution)/shard_map/psum | solution.py:18
  58.1 12.6 %all-reduce.4 = (f32[512,2]{0,1:T(2,128)S(1)}, f32[512,2]{0,1:T(2,128)S(1)}) all-reduce(f32[512,2]{0,1:T(2,128)S(1)} %get-tuple-element.188, f32[512,2]{0,1:T(2,128)S(1)} %get-tuple-element.189), channel_id=1, replica_groups=mesh['blk_0'=8,'blk_1'=4,'grp_0'=2,'grp_1'=4,'grp_2'=2] {'grp_0'}, use_global_device_ids=true, to_apply=%region_22.0 | all-reduce | flops 2048 | bytes 16384 | tf_op jit(solution)/shard_map/psum | solution.py:18
  70.6 9.1 %all-reduce.1 = (f32[512,2]{0,1:T(2,128)S(1)}, f32[512,2]{0,1:T(2,128)S(1)}) all-reduce(f32[512,2]{0,1:T(2,128)S(1)} %get-tuple-element.192, f32[512,2]{0,1:T(2,128)S(1)} %get-tuple-element.193), channel_id=1, replica_groups=mesh['blk_0'=8,'blk_1'=4,'grp_0'=2,'grp_1'=4,'grp_2'=2] {'grp_1'}, use_global_device_ids=true, to_apply=%region_23.24 | all-reduce | flops 2048 | bytes 16384 | tf_op jit(solution)/shard_map/psum | solution.py:18
  79.8 12.2 %all-reduce.3 = (f32[512,2]{0,1:T(2,128)S(1)}, f32[512,2]{0,1:T(2,128)S(1)}) all-reduce(f32[512,2]{0,1:T(2,128)S(1)} %get-tuple-element.186, f32[512,2]{0,1:T(2,128)S(1)} %get-tuple-element.187), channel_id=1, replica_groups=mesh['blk_0'=8,'blk_1'=4,'grp_0'=2,'grp_1'=4,'grp_2'=2] {'grp_2'}, use_global_device_ids=true, to_apply=%region_24.25 | all-reduce | flops 2048 | bytes 16384 | tf_op jit(solution)/shard_map/psum | solution.py:18
  92.0 0.4 fusion.62
  92.4 0.4 convolution_subtract_fusion.1
  93.0 0.2 copy-done.1
  93.1 53.9 %all-gather.1 = f32[8,3,64]{2,1,0:T(4,128)S(1)} all-gather(f32[1,3,64]{2,1,0:T(4,128)S(1)} %bitcast.166), channel_id=2, replica_groups=mesh['blk_0'=8,'blk_1'=4,'grp_0'=2,'grp_1'=4,'grp_2'=2] {'grp_0','grp_1'}, dimensions={0}, use_global_device_ids=true | all-gather | bytes 6912 | tf_op jit(solution)/shard_map/all_gather | solution.py:31
  147.0 6.4 %all_gather.7 = f32[16,3,64]{2,0,1:T(8,128)S(1)} all-gather(f32[8,3,64]{2,0,1:T(8,128)S(1)} %copy.41), channel_id=1, replica_groups=mesh['blk_0'=8,'blk_1'=4,'grp_0'=2,'grp_1'=4,'grp_2'=2] {'grp_2'}, dimensions={0}, use_global_device_ids=true | all-gather | bytes 18432 | tf_op jit(solution)/shard_map/all_gather | solution.py:31
  153.6 0.4 fusion.61
  154.0 0.6 broadcast.270
  154.6 0.9 reduce
  155.7 0.1 split.13
  155.9 79.1 %while.16 = (s32[]{:T(128)}, f32[12,1024]{1,0:T(8,128)S(1)}, f32[3,1024]{1,0:T(4,128)S(1)}, f32[3,2048]{1,0:T(4,128)S(1)}, f32[12,2048]{1,0:T(8,128)S(1)}, /*ind...) while((s32[]{:T(128)}, f32[12,1024]{1,0:T(8,128)S(1)}, ...), condition=%wide.region_13.0_spmd.clone, body=%wide.region_0.13_spmd.clone.sunk | while | flops 36712464 | bytes 378273 | solution.py:175
  156.0 0.1 constant_dynamic-slice_fusion.3
  156.1 9.6 %fusion.77 = (f32[1024]{0:T(1024)S(1)}, f32[1024]{0:T(1024)S(1)}, f32[1024]{0:T(1024)S(1)}, f32[1024]{0:T(1024)S(1)}, f32[1024]{0:T(1024)S(1)}, /*index=5*/f32[1...) fusion(f32[256]{0:T(256)S(1)} %bitcast.160, ...), kind=kLoop, calls=%fused_computation.76.clone.1 | loop fusion | flops 36687872 | bytes 76800 | tf_op jit(solution)/shard_map/while/body/eval_jaxpr/reduce_sum | solution.py:110
  165.8 0.1 constant_dynamic-slice_fusion.3
  166.0 9.6 %fusion.77 = (f32[1024]{0:T(1024)S(1)}, f32[1024]{0:T(1024)S(1)}, f32[1024]{0:T(1024)S(1)}, f32[1024]{0:T(1024)S(1)}, f32[1024]{0:T(1024)S(1)}, /*index=5*/f32[1...) fusion(f32[256]{0:T(256)S(1)} %bitcast.160, ...), kind=kLoop, calls=%fused_computation.76.clone.1 | loop fusion | flops 36687872 | bytes 76800 | tf_op jit(solution)/shard_map/while/body/eval_jaxpr/reduce_sum | solution.py:110
  175.6 0.1 stack.162
  175.7 0.1 constant_dynamic-slice_fusion.3
  175.9 9.6 %fusion.77 = (f32[1024]{0:T(1024)S(1)}, f32[1024]{0:T(1024)S(1)}, f32[1024]{0:T(1024)S(1)}, f32[1024]{0:T(1024)S(1)}, f32[1024]{0:T(1024)S(1)}, /*index=5*/f32[1...) fusion(f32[256]{0:T(256)S(1)} %bitcast.160, ...), kind=kLoop, calls=%fused_computation.76.clone.1 | loop fusion | flops 36687872 | bytes 76800 | tf_op jit(solution)/shard_map/while/body/eval_jaxpr/reduce_sum | solution.py:110
  185.6 0.1 constant_dynamic-slice_fusion.3
  185.8 9.6 %fusion.77 = (f32[1024]{0:T(1024)S(1)}, f32[1024]{0:T(1024)S(1)}, f32[1024]{0:T(1024)S(1)}, f32[1024]{0:T(1024)S(1)}, f32[1024]{0:T(1024)S(1)}, /*index=5*/f32[1...) fusion(f32[256]{0:T(256)S(1)} %bitcast.160, ...), kind=kLoop, calls=%fused_computation.76.clone.1 | loop fusion | flops 36687872 | bytes 76800 | tf_op jit(solution)/shard_map/while/body/eval_jaxpr/reduce_sum | solution.py:110
  195.3 0.1 stack.162
  195.5 0.1 constant_dynamic-slice_fusion.3
  195.6 9.6 %fusion.77 = (f32[1024]{0:T(1024)S(1)}, f32[1024]{0:T(1024)S(1)}, f32[1024]{0:T(1024)S(1)}, f32[1024]{0:T(1024)S(1)}, f32[1024]{0:T(1024)S(1)}, /*index=5*/f32[1...) fusion(f32[256]{0:T(256)S(1)} %bitcast.160, ...), kind=kLoop, calls=%fused_computation.76.clone.1 | loop fusion | flops 36687872 | bytes 76800 | tf_op jit(solution)/shard_map/while/body/eval_jaxpr/reduce_sum | solution.py:110
  205.4 0.1 constant_dynamic-slice_fusion.3
  205.5 9.6 %fusion.77 = (f32[1024]{0:T(1024)S(1)}, f32[1024]{0:T(1024)S(1)}, f32[1024]{0:T(1024)S(1)}, f32[1024]{0:T(1024)S(1)}, f32[1024]{0:T(1024)S(1)}, /*index=5*/f32[1...) fusion(f32[256]{0:T(256)S(1)} %bitcast.160, ...), kind=kLoop, calls=%fused_computation.76.clone.1 | loop fusion | flops 36687872 | bytes 76800 | tf_op jit(solution)/shard_map/while/body/eval_jaxpr/reduce_sum | solution.py:110
  215.3 0.1 constant_dynamic-slice_fusion.3
  215.4 9.6 %fusion.77 = (f32[1024]{0:T(1024)S(1)}, f32[1024]{0:T(1024)S(1)}, f32[1024]{0:T(1024)S(1)}, f32[1024]{0:T(1024)S(1)}, f32[1024]{0:T(1024)S(1)}, /*index=5*/f32[1...) fusion(f32[256]{0:T(256)S(1)} %bitcast.160, ...), kind=kLoop, calls=%fused_computation.76.clone.1 | loop fusion | flops 36687872 | bytes 76800 | tf_op jit(solution)/shard_map/while/body/eval_jaxpr/reduce_sum | solution.py:110
  225.1 0.1 constant_dynamic-slice_fusion.3
  225.3 9.6 %fusion.77 = (f32[1024]{0:T(1024)S(1)}, f32[1024]{0:T(1024)S(1)}, f32[1024]{0:T(1024)S(1)}, f32[1024]{0:T(1024)S(1)}, f32[1024]{0:T(1024)S(1)}, /*index=5*/f32[1...) fusion(f32[256]{0:T(256)S(1)} %bitcast.160, ...), kind=kLoop, calls=%fused_computation.76.clone.1 | loop fusion | flops 36687872 | bytes 76800 | tf_op jit(solution)/shard_map/while/body/eval_jaxpr/reduce_sum | solution.py:110
  235.1 0.7 reshape.65
  235.9 7.9 %all-to-all-start.1 = ((f32[16,1,768]{2,1,0:T(1,128)}), f32[16,1,768]{2,1,0:T(1,128)S(1)}, u32[]{:S(2)}, u32[]{:S(2)}) async-start(f32[16,1,768]{2,1,0:T(1,128)} %reshape.65), calls=%async_computation.1 | async-start | bytes 98304 | tf_op jit(solution)/shard_map/all_to_all | solution.py:69
  243.8 0.4 convolution_add_fusion.1
  244.3 14.0 %all-to-all-done.1 = f32[16,1,768]{2,1,0:T(1,128)S(1)} async-done(((f32[16,1,768]{2,1,0:T(1,128)}), f32[16,1,768]{2,1,0:T(1,128)S(1)}, u32[]{:S(2)}, u32[]{:S(2)}) %all-to-all-start.1) | async-done | bytes 49184 | tf_op jit(solution)/shard_map/all_to_all | solution.py:69
  258.3 0.7 reduce.1
  259.3 0.6 copy-done.4
  259.9 0.6 copy.50
  (60 shorter events, 1.9 us)
Async XLA Ops:
  0.0 18.3 %copy-start = (f32[2,3,64,512]{3,2,1,0:T(8,128)S(1)}, f32[2,3,64,512]{3,2,1,0:T(8,128)}, u32[]{:S(2)}) copy-start(f32[2,3,64,512]{3,2,1,0:T(8,128)} %param.13) | copy-start | bytes 2359300
  2.3 151.6 %all-to-all-start = ((f32[32,1,960]{2,1,0:T(1,128)}), f32[32,1,960]{2,1,0:T(1,128)S(1)}, u32[]{:S(2)}, u32[]{:S(2)}) async-start(f32[32,1,960]{2,1,0:T(1,128)} %reshape.63), calls=%async_computation | async-start | bytes 262144 | tf_op jit(solution)/shard_map/all_to_all | solution.py:44
  79.8 12.2 %copy-start.2 = (f32[512]{0:T(512)S(1)}, f32[512]{0:T(512)}, u32[]{:S(2)}) copy-start(f32[512]{0:T(512)} %param.14) | copy-start | bytes 6148
  79.8 12.2 %copy-start.3 = (f32[512]{0:T(512)S(1)}, f32[512]{0:T(512)}, u32[]{:S(2)}) copy-start(f32[512]{0:T(512)} %param.15) | copy-start | bytes 6148
  92.4 0.7 copy-start.1
  235.9 22.5 %all-to-all-start.1 = ((f32[16,1,768]{2,1,0:T(1,128)}), f32[16,1,768]{2,1,0:T(1,128)S(1)}, u32[]{:S(2)}, u32[]{:S(2)}) async-start(f32[16,1,768]{2,1,0:T(1,128)} %reshape.65), calls=%async_computation.1 | async-start | bytes 98304 | tf_op jit(solution)/shard_map/all_to_all | solution.py:69
  259.2 0.7 copy-start.4
  259.3 0.7 copy-start.5
where the time goes:
time: 261 us
  blocking collectives  133 us (51%)
  other arithmetic  79.1 us (30%)
  starting transfers between devices  23.9 us (9%)
  waiting for transfers between devices  14 us (5%)
  local copies, waits for them, and re-layouts  7.4 us (3%)
  matrix products  2.91 us (1%)
    reduce_sum x8, other arithmetic, pair_field(): jnp.sum(entry_tile, axis=axis_sum)  76.6 us
    psum x5, blocking collectives, over_axes(): value = lax.psum(value, axis)  72.2 us
    all_gather x2, blocking collectives, gather_in_order(): tiles = lax.all_gather(tiles, axes[k], axis=0, tiled=True)  60.3 us
    all_to_all x1, starting transfers between devices, sent_to_all(): lax.all_to_all(jnp.broadcast_to(value[None], (devices, *value.shape)), ax...  15.9 us
    all_to_all x1, waiting for transfers between devices, sent_and_summed(): lax.all_to_all(tiles, axis, split_axis=0, concat_axis=0, tiled=True)  14 us
    all_to_all x1, starting transfers between devices, sent_and_summed(): lax.all_to_all(tiles, axis, split_axis=0, concat_axis=0, tiled=True)  7.95 us
  transfers between devices with their start and end apart: 2, of which 1 were waited for; matrix products, arithmetic and copies ran while one was open for 1% of the time, Pallas kernels for 0%

commit v1 on v0

--- a/solution.py
+++ b/solution.py
@@ -28,7 +28,8 @@
 def gather_in_order(value, axes, sequence):
     tiles = value[None]
     for k in sequence:
-        tiles = lax.all_gather(tiles, axes[k], axis=0, tiled=True)
+        repeated = jnp.stack([tiles] * lax.axis_size(axes[k]))
+        tiles = jnp.concatenate(lax.all_to_all(repeated, axes[k], 0, 0), axis=0)
     block = [lax.axis_size(axes[k]) for k in reversed(sequence)]
     tiles = tiles.reshape(*block, *value.shape)
     turned = sorted(range(len(sequence)), key=lambda place: sequence[len(sequence) - 1 - place])

time: 261 us -> 227 us (0.87)
  blocking collectives: 133 us -> 71.3 us
  starting transfers between devices: 23.9 us -> 36.7 us
  waiting for transfers between devices: 14 us -> 24.3 us
    all_gather x2 -> x0, blocking collectives: 60.3 us -> none  [gather_in_order(): tiles = lax.all_gather(tiles, axes[k], axis=0, tiled=True)]
    all_to_all x0 -> x1, starting transfers between devices: none -> 18.4 us  [gather_in_order(): tiles = jnp.concatenate(lax.all_to_all(repeated, axes[k], 0, 0), axis=0)]
    all_to_all x1, starting transfers between devices: 15.9 us -> 3.85 us  [sent_to_all(): lax.all_to_all(jnp.broadcast_to(value[None], (devices, *value.shape)), ax...]
    all_to_all x1, waiting for transfers between devices: 0.01 us -> 10.3 us  [sent_to_all(): lax.all_to_all(jnp.broadcast_to(value[None], (devices, *value.shape)), ax...]
    all_to_all x1, starting transfers between devices: 7.95 us -> 14.5 us  [sent_and_summed(): lax.all_to_all(tiles, axis, split_axis=0, concat_axis=0, tiled=True)]
    psum x5, blocking collectives: 72.2 us -> 67.6 us  [over_axes(): value = lax.psum(value, axis)]
    all_to_all x0 -> x1, blocking collectives: none -> 3.72 us  [gather_in_order(): tiles = jnp.concatenate(lax.all_to_all(repeated, axes[k], 0, 0), axis=0)]
  transfers between devices with their start and end apart: 2 -> 3, of which waited for: 1 -> 2; matrix products, arithmetic and copies ran while one was open for 1% -> 3% of each run, Pallas kernels for 0% -> 0%
where the time goes in v1:
time: 227 us; the launch traced here: 226 us
  other arithmetic  80.7 us (36%)
  blocking collectives  71.3 us (31%)
  starting transfers between devices  36.7 us (16%)
  waiting for transfers between devices  24.3 us (11%)
  local copies, waits for them, and re-layouts  9.43 us (4%)
  matrix products  2.89 us (1%)
    reduce_sum x8, other arithmetic, pair_field(): jnp.sum(entry_tile, axis=axis_sum)  76.6 us
    psum x5, blocking collectives, over_axes(): value = lax.psum(value, axis)  67.6 us
    all_to_all x1, starting transfers between devices, gather_in_order(): tiles = jnp.concatenate(lax.all_to_all(repeated, axes[k], 0, 0), axis=0)  18.4 us
    all_to_all x1, starting transfers between devices, sent_and_summed(): lax.all_to_all(tiles, axis, split_axis=0, concat_axis=0, tiled=True)  14.5 us
    all_to_all x1, waiting for transfers between devices, sent_and_summed(): lax.all_to_all(tiles, axis, split_axis=0, concat_axis=0, tiled=True)  14 us
    all_to_all x1, waiting for transfers between devices, sent_to_all(): lax.all_to_all(jnp.broadcast_to(value[None], (devices, *value.shape)), ax...  10.3 us
    unnamed x23, local copies, waits for them, and re-layouts  4.88 us
  transfers between devices with their start and end apart: 3, of which 2 were waited for; matrix products, arithmetic and copies ran while one was open for 3% of the time, Pallas kernels for 0%

profile of v1, /device:TPU:1, one launch (start us, length us, event | category | flops | bytes accessed | tf_op | source)
XLA Modules:
  0.0 226.1 jit_solution(11723145948368241598)
XLA Ops:
  0.0 0.7 broadcast_bitcast_fusion
  0.7 0.6 broadcast.272
  1.3 0.7 reduce
  2.0 0.7 reshape.57
  2.7 18.4 %all-to-all-start = ((f32[8,1,192]{2,1,0:T(1,128)}), f32[8,1,192]{2,1,0:T(1,128)S(1)}, u32[]{:S(2)}, u32[]{:S(2)}) async-start(f32[8,1,192]{2,1,0:T(1,128)} %reshape.57), calls=%async_computation | async-start | bytes 16384 | tf_op jit(solution)/shard_map/all_to_all | solution.py:32
  21.2 1.2 fusion.64
  22.4 0.3 fusion.49
  22.7 0.3 fusion.53
  23.0 0.3 convolution_add_fusion
  23.3 0.3 convolution_subtract_fusion
  23.7 25.6 %all-reduce = (f32[512,2]{0,1:T(2,128)S(1)}, f32[512,2]{0,1:T(2,128)S(1)}) all-reduce(f32[512,2]{0,1:T(2,128)S(1)} %convolution_add_fusion, f32[512,2]{0,1:T(2,128)S(1)} %convolution_subtract_fusion), channel_id=1, replica_groups=mesh['blk_0'=8,'blk_1'=4,'grp_0'=2,'grp_1'=4,'grp_2'=2] {'blk_0'}, use_global_device_ids=true, to_apply=%region_20.0 | all-reduce | flops 2048 | bytes 16384 | tf_op jit(solution)/shard_map/psum | solution.py:18
  49.3 8.6 %all-reduce.2 = (f32[512,2]{0,1:T(2,128)S(1)}, f32[512,2]{0,1:T(2,128)S(1)}) all-reduce(f32[512,2]{0,1:T(2,128)S(1)} %get-tuple-element.184, f32[512,2]{0,1:T(2,128)S(1)} %get-tuple-element.185), channel_id=1, replica_groups=mesh['blk_0'=8,'blk_1'=4,'grp_0'=2,'grp_1'=4,'grp_2'=2] {'blk_1'}, use_global_device_ids=true, to_apply=%region_21.0 | all-reduce | flops 2048 | bytes 16384 | tf_op jit(solution)/shard_map/psum | solution.py:18
  57.9 12.6 %all-reduce.4 = (f32[512,2]{0,1:T(2,128)S(1)}, f32[512,2]{0,1:T(2,128)S(1)}) all-reduce(f32[512,2]{0,1:T(2,128)S(1)} %get-tuple-element.188, f32[512,2]{0,1:T(2,128)S(1)} %get-tuple-element.189), channel_id=1, replica_groups=mesh['blk_0'=8,'blk_1'=4,'grp_0'=2,'grp_1'=4,'grp_2'=2] {'grp_0'}, use_global_device_ids=true, to_apply=%region_22.0 | all-reduce | flops 2048 | bytes 16384 | tf_op jit(solution)/shard_map/psum | solution.py:18
  70.5 9.1 %all-reduce.1 = (f32[512,2]{0,1:T(2,128)S(1)}, f32[512,2]{0,1:T(2,128)S(1)}) all-reduce(f32[512,2]{0,1:T(2,128)S(1)} %get-tuple-element.192, f32[512,2]{0,1:T(2,128)S(1)} %get-tuple-element.193), channel_id=1, replica_groups=mesh['blk_0'=8,'blk_1'=4,'grp_0'=2,'grp_1'=4,'grp_2'=2] {'grp_1'}, use_global_device_ids=true, to_apply=%region_23.24 | all-reduce | flops 2048 | bytes 16384 | tf_op jit(solution)/shard_map/psum | solution.py:18
  79.6 11.7 %all-reduce.3 = (f32[512,2]{0,1:T(2,128)S(1)}, f32[512,2]{0,1:T(2,128)S(1)}) all-reduce(f32[512,2]{0,1:T(2,128)S(1)} %get-tuple-element.186, f32[512,2]{0,1:T(2,128)S(1)} %get-tuple-element.187), channel_id=1, replica_groups=mesh['blk_0'=8,'blk_1'=4,'grp_0'=2,'grp_1'=4,'grp_2'=2] {'grp_2'}, use_global_device_ids=true, to_apply=%region_24.25 | all-reduce | flops 2048 | bytes 16384 | tf_op jit(solution)/shard_map/psum | solution.py:18
  91.3 0.4 fusion.62
  91.7 0.3 copy-done
  92.0 0.8 reshape.61
  92.9 0.7 reduce.1
  93.8 3.7 %all_to_all.20 = f32[2,1,1536]{2,1,0:T(1,128)S(1)} all-to-all(f32[2,1,1536]{2,1,0:T(1,128)S(1)} %reshape.59), channel_id=1, replica_groups=mesh['blk_0'=8,'blk_1'=4,'grp_0'=2,'grp_1'=4,'grp_2'=2] {'grp_2'}, dimensions={0} | all-to-all | bytes 24576 | tf_op jit(solution)/shard_map/all_to_all | solution.py:32
  97.5 3.9 %all-to-all-start.2 = ((f32[32,1,960]{2,1,0:T(1,128)}), f32[32,1,960]{2,1,0:T(1,128)S(1)}, u32[]{:S(2)}, u32[]{:S(2)}) async-start(f32[32,1,960]{2,1,0:T(1,128)} %reshape.61), calls=%async_computation.2 | async-start | bytes 262144 | tf_op jit(solution)/shard_map/all_to_all | solution.py:45
  101.4 0.4 convolution_subtract_fusion.1
  101.9 0.4 fusion.61
  102.3 0.7 reduce.2
  103.3 10.3 %all-to-all-done.2 = f32[32,1,960]{2,1,0:T(1,128)S(1)} async-done(((f32[32,1,960]{2,1,0:T(1,128)}), f32[32,1,960]{2,1,0:T(1,128)S(1)}, u32[]{:S(2)}, u32[]{:S(2)}) %all-to-all-start.2) | async-done | bytes 122912 | tf_op jit(solution)/shard_map/all_to_all | solution.py:45
  113.5 1.0 reduce.3
  115.0 79.1 %while.16 = (s32[]{:T(128)}, f32[12,1024]{1,0:T(8,128)S(1)}, f32[3,1024]{1,0:T(4,128)S(1)}, f32[3,2048]{1,0:T(4,128)S(1)}, f32[12,2048]{1,0:T(8,128)S(1)}, /*ind...) while((s32[]{:T(128)}, f32[12,1024]{1,0:T(8,128)S(1)}, ...), condition=%wide.region_13.0_spmd.clone, body=%wide.region_0.13_spmd.clone.sunk | while | flops 36712464 | bytes 378273 | solution.py:176
  115.0 0.1 constant_dynamic-slice_fusion.3
  115.1 9.6 %fusion.77 = (f32[1024]{0:T(1024)S(1)}, f32[1024]{0:T(1024)S(1)}, f32[1024]{0:T(1024)S(1)}, f32[1024]{0:T(1024)S(1)}, f32[1024]{0:T(1024)S(1)}, /*index=5*/f32[1...) fusion(f32[256]{0:T(256)S(1)} %bitcast.169, ...), kind=kLoop, calls=%fused_computation.76.clone.1 | loop fusion | flops 36687872 | bytes 76800 | tf_op jit(solution)/shard_map/while/body/eval_jaxpr/reduce_sum | solution.py:111
  124.9 0.1 constant_dynamic-slice_fusion.3
  125.0 9.6 %fusion.77 = (f32[1024]{0:T(1024)S(1)}, f32[1024]{0:T(1024)S(1)}, f32[1024]{0:T(1024)S(1)}, f32[1024]{0:T(1024)S(1)}, f32[1024]{0:T(1024)S(1)}, /*index=5*/f32[1...) fusion(f32[256]{0:T(256)S(1)} %bitcast.169, ...), kind=kLoop, calls=%fused_computation.76.clone.1 | loop fusion | flops 36687872 | bytes 76800 | tf_op jit(solution)/shard_map/while/body/eval_jaxpr/reduce_sum | solution.py:111
  134.7 0.1 constant_dynamic-slice_fusion.3
  134.9 9.6 %fusion.77 = (f32[1024]{0:T(1024)S(1)}, f32[1024]{0:T(1024)S(1)}, f32[1024]{0:T(1024)S(1)}, f32[1024]{0:T(1024)S(1)}, f32[1024]{0:T(1024)S(1)}, /*index=5*/f32[1...) fusion(f32[256]{0:T(256)S(1)} %bitcast.169, ...), kind=kLoop, calls=%fused_computation.76.clone.1 | loop fusion | flops 36687872 | bytes 76800 | tf_op jit(solution)/shard_map/while/body/eval_jaxpr/reduce_sum | solution.py:111
  144.6 0.1 constant_dynamic-slice_fusion.3
  144.8 9.6 %fusion.77 = (f32[1024]{0:T(1024)S(1)}, f32[1024]{0:T(1024)S(1)}, f32[1024]{0:T(1024)S(1)}, f32[1024]{0:T(1024)S(1)}, f32[1024]{0:T(1024)S(1)}, /*index=5*/f32[1...) fusion(f32[256]{0:T(256)S(1)} %bitcast.169, ...), kind=kLoop, calls=%fused_computation.76.clone.1 | loop fusion | flops 36687872 | bytes 76800 | tf_op jit(solution)/shard_map/while/body/eval_jaxpr/reduce_sum | solution.py:111
  154.5 0.1 constant_dynamic-slice_fusion.3
  154.7 9.6 %fusion.77 = (f32[1024]{0:T(1024)S(1)}, f32[1024]{0:T(1024)S(1)}, f32[1024]{0:T(1024)S(1)}, f32[1024]{0:T(1024)S(1)}, f32[1024]{0:T(1024)S(1)}, /*index=5*/f32[1...) fusion(f32[256]{0:T(256)S(1)} %bitcast.169, ...), kind=kLoop, calls=%fused_computation.76.clone.1 | loop fusion | flops 36687872 | bytes 76800 | tf_op jit(solution)/shard_map/while/body/eval_jaxpr/reduce_sum | solution.py:111
  164.5 9.6 %fusion.77 = (f32[1024]{0:T(1024)S(1)}, f32[1024]{0:T(1024)S(1)}, f32[1024]{0:T(1024)S(1)}, f32[1024]{0:T(1024)S(1)}, f32[1024]{0:T(1024)S(1)}, /*index=5*/f32[1...) fusion(f32[256]{0:T(256)S(1)} %bitcast.169, ...), kind=kLoop, calls=%fused_computation.76.clone.1 | loop fusion | flops 36687872 | bytes 76800 | tf_op jit(solution)/shard_map/while/body/eval_jaxpr/reduce_sum | solution.py:111
  174.4 9.6 %fusion.77 = (f32[1024]{0:T(1024)S(1)}, f32[1024]{0:T(1024)S(1)}, f32[1024]{0:T(1024)S(1)}, f32[1024]{0:T(1024)S(1)}, f32[1024]{0:T(1024)S(1)}, /*index=5*/f32[1...) fusion(f32[256]{0:T(256)S(1)} %bitcast.169, ...), kind=kLoop, calls=%fused_computation.76.clone.1 | loop fusion | flops 36687872 | bytes 76800 | tf_op jit(solution)/shard_map/while/body/eval_jaxpr/reduce_sum | solution.py:111
  184.2 0.1 constant_dynamic-slice_fusion.3
  184.3 9.6 %fusion.77 = (f32[1024]{0:T(1024)S(1)}, f32[1024]{0:T(1024)S(1)}, f32[1024]{0:T(1024)S(1)}, f32[1024]{0:T(1024)S(1)}, f32[1024]{0:T(1024)S(1)}, /*index=5*/f32[1...) fusion(f32[256]{0:T(256)S(1)} %bitcast.169, ...), kind=kLoop, calls=%fused_computation.76.clone.1 | loop fusion | flops 36687872 | bytes 76800 | tf_op jit(solution)/shard_map/while/body/eval_jaxpr/reduce_sum | solution.py:111
  194.2 0.7 reshape.63
  194.9 14.5 %all-to-all-start.3 = ((f32[16,1,768]{2,1,0:T(1,128)}), f32[16,1,768]{2,1,0:T(1,128)S(1)}, u32[]{:S(2)}, u32[]{:S(2)}) async-start(f32[16,1,768]{2,1,0:T(1,128)} %reshape.63), calls=%async_computation.3 | async-start | bytes 98304 | tf_op jit(solution)/shard_map/all_to_all | solution.py:70
  209.4 0.4 convolution_add_fusion.1
  209.9 14.0 %all-to-all-done.3 = f32[16,1,768]{2,1,0:T(1,128)S(1)} async-done(((f32[16,1,768]{2,1,0:T(1,128)}), f32[16,1,768]{2,1,0:T(1,128)S(1)}, u32[]{:S(2)}, u32[]{:S(2)}) %all-to-all-start.3) | async-done | bytes 49184 | tf_op jit(solution)/shard_map/all_to_all | solution.py:70
  223.9 0.8 reduce.4
  224.9 0.6 copy-done.4
  225.5 0.6 copy.60
  (72 shorter events, 2.7 us)
Async XLA Ops:
  2.7 18.4 %copy-start.1 = (f32[2,2,3,64]{3,1,2,0:T(2,128)S(1)}, f32[2,2,3,64]{3,1,2,0:T(2,128)}, u32[]{:S(2)}) copy-start(f32[2,2,3,64]{3,1,2,0:T(2,128)} %param.10) | copy-start | bytes 9220
  2.7 90.2 %all-to-all-start = ((f32[8,1,192]{2,1,0:T(1,128)}), f32[8,1,192]{2,1,0:T(1,128)S(1)}, u32[]{:S(2)}, u32[]{:S(2)}) async-start(f32[8,1,192]{2,1,0:T(1,128)} %reshape.57), calls=%async_computation | async-start | bytes 16384 | tf_op jit(solution)/shard_map/all_to_all | solution.py:32
  79.6 11.7 %copy-start.2 = (f32[512]{0:T(512)S(1)}, f32[512]{0:T(512)}, u32[]{:S(2)}) copy-start(f32[512]{0:T(512)} %param.14) | copy-start | bytes 6148
  79.6 11.7 %copy-start.3 = (f32[512]{0:T(512)S(1)}, f32[512]{0:T(512)}, u32[]{:S(2)}) copy-start(f32[512]{0:T(512)} %param.15) | copy-start | bytes 6148
  91.3 0.7 copy-start
  97.5 16.0 %all-to-all-start.2 = ((f32[32,1,960]{2,1,0:T(1,128)}), f32[32,1,960]{2,1,0:T(1,128)S(1)}, u32[]{:S(2)}, u32[]{:S(2)}) async-start(f32[32,1,960]{2,1,0:T(1,128)} %reshape.61), calls=%async_computation.2 | async-start | bytes 262144 | tf_op jit(solution)/shard_map/all_to_all | solution.py:45
  194.9 29.0 %all-to-all-start.3 = ((f32[16,1,768]{2,1,0:T(1,128)}), f32[16,1,768]{2,1,0:T(1,128)S(1)}, u32[]{:S(2)}, u32[]{:S(2)}) async-start(f32[16,1,768]{2,1,0:T(1,128)} %reshape.63), calls=%async_computation.3 | async-start | bytes 98304 | tf_op jit(solution)/shard_map/all_to_all | solution.py:70
  224.8 0.7 copy-start.4
  224.9 0.7 copy-start.5
